TPU v7x, 32 devices: a whole 2x2x4 slice. The times are simulated.
32 devices in a mesh: grp: 4 (over x, core), dom: 8 (over z, y).
Axes of the slice: x: 2, y: 2, z: 4, core: 2. Of those that a mesh axis runs over, the one named last changes fastest.
Arguments:
- tracers: float32 [2, 80, 262144], P(None, None, ('grp', 'dom')), may hold values from -6 to 6
- mix_weights: float32 [6, 262144], P(None, ('grp', 'dom')), may hold values from 0 to 0.16
- neighbors: int32 [6, 262144], P(None, ('grp', 'dom')), may hold values from 0 to 10239
- send_list: int32 [65536], P(('grp', 'dom')), may hold values from 0 to 8191
- slot_cell: int32 [65536], P(('grp', 'dom')), may hold values from 0 to 8191
- slot_owner: int32 [65536, 1], P(('grp', 'dom')), may hold values from 0 to 31; in each aligned block of 2048 rows (0 to 2047, 2048 to 4095, ...) at most 128 rows name the same one
- slot_node: int32 [65536], P(('grp', 'dom')), may hold values from 0 to 4095
- thickness: float32 [128, 1024], P('dom', 'grp'), may hold values from 0.6 to 1.9
- friction: float32 [128, 1024], P('dom', 'grp'), may hold values from 0.2 to 2
- driving: float32 [128, 1024], P('dom', 'grp'), may hold values from -6 to 6
- velocity: float32 [128, 1024], P('dom', 'grp'), may hold values from -4 to 4
Outputs:
- ocean_state: float32 [2, 80, 262144], P(None, None, ('grp', 'dom'))
- ice_thickness: float32 [128, 1024], P('dom', 'grp')
- ice_velocity: float32 [128, 1024], P('dom', 'grp')
Inputs may be any that keep to these rules, and one draw needn't show every extreme that they name: `slot_owner`: among the 2048 slots of one block at most 128 name the same owner, a bound that some block reaches.
All inputs are finite; a program needn't handle non-finite values.
Results may differ from a plain program's by a relative error of at most 0.0033.
Values sent between devices are 32-bit elements; how exact they have to be, the bound alone decides.
A program may use at most 192 MiB of HBM per device.

v0:
```python
import jax
import jax.numpy as jnp
from jax import lax
from jax.sharding import PartitionSpec as P

ITERS = 4


VERT_MIX = 0.2
COLUMN_DEPTH = 2.0
SPREAD_INV = 3.0
DRAFT_RATIO = 0.89
FREEZE_SALT = 0.0573
FREEZE_DEPTH = 0.76
THIN_RATE = 0.05
HEAT_SINK = 12.0
SALT_SINK = 6.0
VISC_FLOOR = 0.05


def with_halo(block, sides, width, periodic):
    for axis, dim in sides:
        count = lax.axis_size(axis)
        forward = [(i, i + 1) for i in range(count - 1)]
        if periodic:
            forward.append((count - 1, 0))
        backward = [(target, source) for source, target in forward]
        low = lax.ppermute(
            lax.slice_in_dim(block, block.shape[dim] - width, None, axis=dim), axis, forward
        )
        high = lax.ppermute(lax.slice_in_dim(block, 0, width, axis=dim), axis, backward)
        block = jnp.concatenate([low, block, high], axis=dim)
    return block


def vertical_mix(quantity):
    shifted_up = jnp.concatenate([quantity[:, :1], quantity[:, :-1]], axis=1)
    shifted_down = jnp.concatenate([quantity[:, 1:], quantity[:, -1:]], axis=1)
    return shifted_up + shifted_down - 2.0 * quantity


def level_share_cols(depths, levels):
    centers = (jnp.arange(levels, dtype=jnp.float32) + 0.5) * (COLUMN_DEPTH / levels)
    kernel = jnp.exp(-SPREAD_INV * (centers[:, None] - depths[None, :]) ** 2)
    return kernel / jnp.sum(kernel, axis=0, keepdims=True)


def melt_cols(heat_cols, salt_cols, depths):
    level_part = level_share_cols(depths, heat_cols.shape[0])
    heat_mean = jnp.sum(level_part * heat_cols, axis=0)
    salt_mean = jnp.sum(level_part * salt_cols, axis=0)
    return (heat_mean - FREEZE_SALT * salt_mean + FREEZE_DEPTH * depths, level_part)


def ice_image(quantity, viscosity, friction, padded, padded_visc):
    northern = padded[2:, 1:-1]
    southern = padded[:-2, 1:-1]
    eastern = padded[1:-1, 2:]
    western = padded[1:-1, :-2]
    west_visc = padded_visc[1:-1, :-2]
    south_visc = padded_visc[:-2, 1:-1]
    image = friction * quantity + viscosity * (2.0 * quantity - eastern - northern)
    image = image + west_visc * (quantity - western) + south_visc * (quantity - southern)
    return (image, west_visc, south_visc)


def local(
    tracers,
    mix_weights,
    neighbors,
    send_list,
    slot_cell,
    slot_owner,
    slot_node,
    thickness,
    friction,
    driving,
    velocity,
):
    levels = tracers.shape[1]
    cell_count = tracers.shape[2]
    groups = lax.axis_size("grp")
    domains = lax.axis_size("dom")
    devices = groups * domains
    slot_count = slot_cell.shape[0]
    capacity = max(2, 2 * slot_count // devices)
    owners = slot_owner[:, 0]
    onehot = (owners[:, None] == jnp.arange(devices, dtype=jnp.int32)[None, :]).astype(jnp.int32)
    earlier = jnp.cumsum(onehot, axis=0) - onehot
    position = jnp.sum(earlier * onehot, axis=1)
    target = owners * capacity + position
    node_slots = jnp.full((devices * capacity,), -1, jnp.int32).at[target].set(slot_node)
    flat_thick = thickness.reshape(-1)
    rim_cells = send_list.shape[0] // 2
    flat_tracers = tracers.reshape(2 * levels, cell_count)
    outgoing = jnp.take(flat_tracers, send_list, axis=1)
    widened = with_halo(outgoing, (("dom", 1),), rim_cells, True)
    extended = jnp.concatenate(
        [flat_tracers, widened[:, :rim_cells], widened[:, 3 * rim_cells :]], axis=1
    )
    horizontal = jnp.zeros_like(flat_tracers)
    for neighbor in range(neighbors.shape[0]):
        gathered = jnp.take(extended, neighbors[neighbor], axis=1)
        horizontal = horizontal + mix_weights[neighbor][None, :] * (gathered - flat_tracers)
    mixed_state = tracers + horizontal.reshape(tracers.shape) + VERT_MIX * vertical_mix(tracers)
    columns = jnp.take(mixed_state, slot_cell, axis=2)
    packed = (
        jnp.zeros((2 * levels, devices * capacity), jnp.float32)
        .at[:, target]
        .set(columns.reshape(2 * levels, slot_count))
    )
    arrived, arrived_nodes = (
        lax.all_to_all(packed, ("grp", "dom"), split_axis=1, concat_axis=1, tiled=True),
        lax.all_to_all(
            node_slots.reshape(1, devices * capacity),
            ("grp", "dom"),
            split_axis=1,
            concat_axis=1,
            tiled=True,
        ),
    )
    received = arrived.reshape(2, levels, devices * capacity)
    node_ids = arrived_nodes.reshape(-1)
    present = node_ids >= 0
    node_safe = jnp.where(present, node_ids, 0)
    depths = DRAFT_RATIO * flat_thick[node_safe]
    melt_rate, level_part = melt_cols(received[0], received[1], depths)
    melt_rate = jnp.where(present, melt_rate, 0.0)
    returned_melt, returned_depth = (
        lax.all_to_all(
            melt_rate.reshape(devices, capacity),
            ("grp", "dom"),
            split_axis=0,
            concat_axis=0,
            tiled=True,
        ),
        lax.all_to_all(
            depths.reshape(devices, capacity),
            ("grp", "dom"),
            split_axis=0,
            concat_axis=0,
            tiled=True,
        ),
    )
    own_melt = returned_melt[owners, position]
    own_depth = returned_depth[owners, position]
    own_share = level_share_cols(own_depth, levels)
    weighted = own_melt[None, :] * own_share
    sink_rates = jnp.array([HEAT_SINK, SALT_SINK], dtype=jnp.float32)
    increments = -sink_rates[:, None, None] * weighted[None]
    ocean_out = mixed_state.at[:, :, slot_cell].add(increments)
    ice_thick = flat_thick.at[node_safe].add(-THIN_RATE * melt_rate).reshape(thickness.shape)
    viscosity = VISC_FLOOR + 0.5 * ice_thick * ice_thick
    forcing = driving * ice_thick

    def operate(quantity):
        stacked = jnp.stack([quantity, viscosity])
        border = with_halo(stacked, (("grp", 2), ("dom", 1)), 1, False)
        return ice_image(quantity, viscosity, friction, border[0], border[1])

    image, west_visc, south_visc = operate(velocity)
    diagonal = friction + 2.0 * viscosity + west_visc + south_visc
    solution = velocity
    residual = forcing - image
    precond = residual / diagonal
    direction = precond
    norm_now = lax.psum(jnp.sum(residual * precond), ("grp", "dom"))
    for sweep in range(ITERS):
        image = operate(direction)[0]
        curvature_sum = lax.psum(jnp.sum(direction * image), ("grp", "dom"))
        step_length = norm_now / curvature_sum
        solution = solution + step_length * direction
        residual = residual - step_length * image
        precond = residual / diagonal
        if sweep + 1 < ITERS:
            norm_next = lax.psum(jnp.sum(residual * precond), ("grp", "dom"))
            direction = precond + norm_next / norm_now * direction
            norm_now = norm_next
    return (ocean_out, ice_thick, solution)


def solution(mesh):
    return jax.shard_map(
        local,
        mesh=mesh,
        in_specs=(
            P(None, None, ("grp", "dom")),
            P(None, ("grp", "dom")),
            P(None, ("grp", "dom")),
            P(("grp", "dom")),
            P(("grp", "dom")),
            P(("grp", "dom"), None),
            P(("grp", "dom")),
            P("dom", "grp"),
            P("dom", "grp"),
            P("dom", "grp"),
            P("dom", "grp"),
        ),
        out_specs=(P(None, None, ("grp", "dom")), P("dom", "grp"), P("dom", "grp")),
        check_vma=False,
    )
```

profile of v0, /device:TPU:1, one launch (start us, length us, event | category | flops | bytes accessed | tf_op | source)
XLA Modules:
  0.0 1118.4 jit_solution(14584031706556307426)
XLA Ops:
  71.7 10.6 pad_maximum_fusion
  82.3 35.4 %gather_fusion.5 = f32[8192,160]{1,0:T(8,128)} fusion(f32[160,10240]{0,1:T(8,128)} %pad_maximum_fusion, s32[8192]{0:T(1024)S(1)} %copy-done.10), kind=kCustom, calls=%fused_computation.clone | custom fusion | bytes 10518528 | tf_op jit(solution)/shard_map/jit(_take)/gather | solution.py:103
  126.0 35.4 %gather_fusion.6 = f32[8192,160]{1,0:T(8,128)} fusion(f32[160,10240]{0,1:T(8,128)} %pad_maximum_fusion, s32[8192]{0:T(1024)S(1)} %copy-done.9), kind=kCustom, calls=%fused_computation.1.clone | custom fusion | bytes 10518528 | tf_op jit(solution)/shard_map/jit(_take)/gather | solution.py:103
  169.7 35.4 %gather_fusion.7 = f32[8192,160]{1,0:T(8,128)} fusion(f32[160,10240]{0,1:T(8,128)} %pad_maximum_fusion, s32[8192]{0:T(1024)S(1)} %copy-done.8), kind=kCustom, calls=%fused_computation.2.clone | custom fusion | bytes 10518528 | tf_op jit(solution)/shard_map/jit(_take)/gather | solution.py:103
  213.3 35.4 %gather_fusion.8 = f32[8192,160]{1,0:T(8,128)} fusion(f32[160,10240]{0,1:T(8,128)} %pad_maximum_fusion, s32[8192]{0:T(1024)S(1)} %copy-done.7), kind=kCustom, calls=%fused_computation.3.clone | custom fusion | bytes 10518528 | tf_op jit(solution)/shard_map/jit(_take)/gather | solution.py:103
  257.0 35.4 %gather_fusion.9 = f32[8192,160]{1,0:T(8,128)} fusion(f32[160,10240]{0,1:T(8,128)} %pad_maximum_fusion, s32[8192]{0:T(1024)S(1)} %copy-done.6), kind=kCustom, calls=%fused_computation.4.clone | custom fusion | bytes 10518528 | tf_op jit(solution)/shard_map/jit(_take)/gather | solution.py:103
  300.7 35.4 %gather_fusion.10 = f32[8192,160]{1,0:T(8,128)} fusion(f32[160,10240]{0,1:T(8,128)} %pad_maximum_fusion, s32[8192]{0:T(1024)S(1)} %copy-done.5), kind=kCustom, calls=%fused_computation.5.clone | custom fusion | bytes 10518528 | tf_op jit(solution)/shard_map/jit(_take)/gather | solution.py:103
  344.6 14.2 %fusion.4 = f32[160,8192]{1,0:T(8,128)S(1)} fusion(f32[8192,160]{0,1:T(8,128)} %copy.163, f32[8192,160]{0,1:T(8,128)} %copy.162, f32[8192,160]{0,1:T(8,128)} %copy.161, f32[8192,160]{0,1:T(8,128)} %copy.160, f32[8192,160]{0,1:T(8,128)} %copy.159, f32[8192,160]{0,1:T(8,128)} %copy.158, f32[8192]{0:T(1024)S(1)} %bitcast.195, f32[8192]{0:T(1024)S(1)} %bitcast.196, ...), kind=kLoop, calls=%fused_computation.22 | loop fusion | flops 30146560 | bytes 42188800 | tf_op jit(solution)/shard_map/add | solution.py:104
  365.9 11.1 copy.172
  389.2 11.4 %scatter_custom_fusion.1 = f32[160,4096]{0,1:T(8,128)} fusion(s32[2048]{0:T(1024)} %bitcast.205, f32[2048,160]{1,0:T(8,128)S(1)} %copy.169, f32[]{:T(128)} %constant.41.clone.1), kind=kCustom, calls=%fused_computation.39 | custom fusion | bytes 2621952 | tf_op jit(solution)/shard_map/scatter | solution.py:110
  412.3 23.0 %gather_fusion.1 = f32[4096]{0:T(1024)S(1)} fusion(f32[4096]{0:T(1024)S(1)} %bitcast.148, s32[4096]{0:T(1024)S(1)} %broadcast_clamp_fusion), kind=kCustom, calls=%fused_computation.7 | custom fusion | bytes 49152 | tf_op jit(solution)/shard_map/gather | solution.py:126
  437.0 35.6 %all-to-all-done.1 = f32[160,32,128]{2,0,1:T(8,128)S(1)} async-done(((f32[160,32,128]{2,0,1:T(8,128)}), f32[160,32,128]{2,0,1:T(8,128)S(1)}, u32[]{:S(2)}, u32[]{:S(2)}) %all-to-all-start.1) | async-done | bytes 2621472 | tf_op jit(solution)/shard_map/all_to_all | solution.py:113
  474.1 26.3 %scatter_fusion.1 = f32[4096]{0:T(1024)S(1)} fusion(f32[4096]{0:T(1024)S(1)} %bitcast.149, s32[4096]{0:T(1024)S(1)} %bitcast.190, f32[4096]{0:T(1024)S(1)} %get-tuple-element.45), kind=kCustom, calls=%fused_computation.14 | custom fusion | flops 4096 | bytes 65536 | tf_op jit(solution)/shard_map/scatter-add | solution.py:152
  531.4 41.0 %all-reduce = (f32[]{:T(128)}, f32[]{:T(128)}) all-reduce(f32[]{:T(128)} %get-tuple-element.28, f32[]{:T(128)} %get-tuple-element.27), channel_id=1, replica_groups=mesh['grp'=4,'dom'=8] {'grp','dom'}, use_global_device_ids=true, to_apply=%region_12.14 | all-reduce | flops 2 | bytes 16 | tf_op jit(solution)/shard_map/psum | solution.py:167
  574.3 39.4 %psum.58 = f32[]{:T(128)} all-reduce(f32[]{:T(128)} %get-tuple-element.38), channel_id=1, replica_groups=mesh['grp'=4,'dom'=8] {'grp','dom'}, use_global_device_ids=true, to_apply=%region_16.18 | all-reduce | flops 1 | bytes 8 | tf_op jit(solution)/shard_map/psum | solution.py:176
  634.0 40.4 %psum.59 = f32[]{:T(128)} all-reduce(f32[]{:T(128)} %get-tuple-element.36), channel_id=1, replica_groups=mesh['grp'=4,'dom'=8] {'grp','dom'}, use_global_device_ids=true, to_apply=%region_18.20 | all-reduce | flops 1 | bytes 8 | tf_op jit(solution)/shard_map/psum | solution.py:170
  676.2 39.1 %psum.60 = f32[]{:T(128)} all-reduce(f32[]{:T(128)} %get-tuple-element.33), channel_id=1, replica_groups=mesh['grp'=4,'dom'=8] {'grp','dom'}, use_global_device_ids=true, to_apply=%region_20.22 | all-reduce | flops 1 | bytes 8 | tf_op jit(solution)/shard_map/psum | solution.py:176
  736.7 39.9 %psum.61 = f32[]{:T(128)} all-reduce(f32[]{:T(128)} %get-tuple-element.31), channel_id=1, replica_groups=mesh['grp'=4,'dom'=8] {'grp','dom'}, use_global_device_ids=true, to_apply=%region_22.24 | all-reduce | flops 1 | bytes 8 | tf_op jit(solution)/shard_map/psum | solution.py:170
  778.5 13.1 %gather_fusion.4 = f32[2048]{0:T(1024)S(1)} fusion(f32[32,128]{1,0:T(8,128)S(1)} %bitcast.150, s32[2048]{0:T(1024)S(1)} %bitcast.152), kind=kCustom, calls=%fused_computation.10 | custom fusion | bytes 32768 | tf_op jit(solution)/shard_map/gather | solution.py:146
  791.6 40.6 %psum.62 = f32[]{:T(128)} all-reduce(f32[]{:T(128)} %multiply_reduce_fusion), channel_id=1, replica_groups=mesh['grp'=4,'dom'=8] {'grp','dom'}, use_global_device_ids=true, to_apply=%region_24.26 | all-reduce | flops 1 | bytes 8 | tf_op jit(solution)/shard_map/psum | solution.py:176
  856.7 39.7 %psum.63 = f32[]{:T(128)} all-reduce(f32[]{:T(128)} %fusion.69), channel_id=1, replica_groups=mesh['grp'=4,'dom'=8] {'grp','dom'}, use_global_device_ids=true, to_apply=%region_26.28 | all-reduce | flops 1 | bytes 8 | tf_op jit(solution)/shard_map/psum | solution.py:170
  898.4 13.1 %gather_fusion.3 = f32[2048]{0:T(1024)S(1)} fusion(f32[32,128]{1,0:T(8,128)S(1)} %bitcast.151, s32[2048]{0:T(1024)S(1)} %bitcast.153), kind=kCustom, calls=%fused_computation.9 | custom fusion | bytes 32768 | tf_op jit(solution)/shard_map/gather | solution.py:145
  913.2 194.0 %scatter_fusion = f32[2,80,8192]{1,0,2:T(2,128)} fusion(f32[2,80,8192]{1,0,2:T(2,128)} %copy.172, s32[2048]{0:T(1024)S(1)} %copy-done.18, f32[2048,2,80]{2,1,0:T(2,128)S(1)} %multiply_bitcast_fusion), kind=kCustom, calls=%fused_computation.13 | custom fusion | flops 327680 | bytes 3940352 | tf_op jit(solution)/shard_map/scatter-add | solution.py:151
  1107.2 11.2 %copy.173 = f32[2,80,8192]{2,1,0:T(8,128)} copy(f32[2,80,8192]{1,0,2:T(2,128)} %scatter_fusion) | data formatting | bytes 10485760
  (214 shorter events, 251.8 us)
Async XLA Ops:
  20.8 49.1 %collective-permute-start = (f32[160,1024]{1,0:T(8,128)S(1)}, f32[160,1024]{1,0:T(8,128)S(1)}, u32[]{:S(2)}, u32[]{:S(2)}) collective-permute-start(f32[160,1024]{1,0:T(8,128)S(1)} %copy.153), channel_id=1, source_target_pairs={{0,1},{1,2},{2,3},{3,4},{4,5},{5,6},{6,7},{7,0},{8,9},{9,10},{10,1... | collective-permute-start | bytes 1966088 | tf_op jit(solution)/shard_map/ppermute | solution.py:28
  23.2 47.0 %collective-permute-start.1 = (f32[160,1024]{1,0:T(8,128)S(1)}, f32[160,1024]{1,0:T(8,128)}, u32[]{:S(2)}, u32[]{:S(2)}) collective-permute-start(f32[160,1024]{1,0:T(8,128)S(1)} %copy.154), channel_id=1, source_target_pairs={{1,0},{2,1},{3,2},{4,3},{5,4},{6,5},{7,6},{0,7},{9,8},{10,9},{11,1... | collective-permute-start | bytes 1966088 | tf_op jit(solution)/shard_map/ppermute | solution.py:31
  45.7 360.0 %all-to-all-start = ((s32[1,32,128]{2,0,1:T(1,128)}), s32[1,32,128]{2,0,1:T(1,128)}, u32[]{:S(2)}, u32[]{:S(2)}) async-start(s32[1,32,128]{2,0,1:T(1,128)} %bitcast.28), calls=%async_computation | async-start | bytes 32768 | tf_op jit(solution)/shard_map/all_to_all | solution.py:114
  405.7 67.0 %all-to-all-start.1 = ((f32[160,32,128]{2,0,1:T(8,128)}), f32[160,32,128]{2,0,1:T(8,128)S(1)}, u32[]{:S(2)}, u32[]{:S(2)}) async-start(f32[160,32,128]{2,0,1:T(8,128)} %copy.170), calls=%async_computation.1 | async-start | bytes 5242880 | tf_op jit(solution)/shard_map/all_to_all | solution.py:113
  500.5 4.7 collective-permute-start.2
  503.3 5.1 collective-permute-start.3
  509.8 4.3 collective-permute-start.5
  514.4 5.0 collective-permute-start.6
  517.5 5.1 collective-permute-start.7
  522.6 4.9 collective-permute-start.8
  526.3 4.3 collective-permute-start.9
  615.1 7.0 collective-permute-start.10
  620.2 5.1 collective-permute-start.11
  628.0 5.1 collective-permute-start.13
  716.7 7.0 collective-permute-start.14
  721.8 5.1 collective-permute-start.15
  726.9 8.9 collective-permute-start.16
  730.7 5.2 collective-permute-start.17
  732.0 46.6 %all-to-all-start.3 = ((f32[32,1,128]{2,1,0:T(1,128)}), f32[32,1,128]{2,1,0:T(1,128)S(1)}, u32[]{:S(2)}, u32[]{:S(2)}) async-start(f32[32,1,128]{2,1,0:T(1,128)} %bitcast.44), calls=%async_computation.3 | async-start | bytes 32768 | tf_op jit(solution)/shard_map/all_to_all | solution.py:137
  833.6 7.7 collective-permute-start.18
  838.7 5.1 collective-permute-start.19
  843.8 5.2 collective-permute-start.20
  847.1 4.3 collective-permute-start.21
  852.3 46.0 %all-to-all-start.2 = ((f32[32,1,128]{2,1,0:T(1,128)}), f32[32,1,128]{2,1,0:T(1,128)S(1)}, u32[]{:S(2)}, u32[]{:S(2)}) async-start(f32[32,1,128]{2,1,0:T(1,128)} %bitcast.41), calls=%async_computation.2 | async-start | bytes 32768 | tf_op jit(solution)/shard_map/all_to_all | solution.py:130
  (34 other events, 1034.0 us)
where the time goes:
time: 1120 us
  local copies, waits for them, and re-layouts  405 us (36%)
  other arithmetic  284 us (25%)
  blocking collectives  280 us (25%)
  starting transfers between devices  75.1 us (7%)
  waiting for transfers between devices  62.9 us (6%)
    gather x12, local copies, waits for them, and re-layouts, local(): gathered = jnp.take(extended, neighbors[neighbor], axis=1)  262 us
    scatter-add x1, other arithmetic, local(): ocean_out = mixed_state.at[:, :, slot_cell].add(increments)  194 us
    psum x3, blocking collectives, local(): curvature_sum = lax.psum(jnp.sum(direction * image), ('grp', 'dom'))  120 us
    psum x3, blocking collectives, local(): norm_next = lax.psum(jnp.sum(residual * precond), ('grp', 'dom'))  119 us
    psum x1, blocking collectives, local(): norm_now = lax.psum(jnp.sum(residual * precond), ('grp', 'dom'))  41 us
    ppermute x11, starting transfers between devices, with_halo(): lax.ppermute(lax.slice_in_dim(block, block.shape[dim] - width, None, axis...  37.8 us
    all_to_all x1, waiting for transfers between devices, local(): lax.all_to_all(packed, ('grp', 'dom'), split_axis=1, concat_axis=1, tiled...  35.6 us
    ppermute x11, waiting for transfers between devices, with_halo(): lax.ppermute(lax.slice_in_dim(block, 0, width, axis=dim), axis, backward)  27.2 us
  transfers between devices with their start and end apart: 26, of which 10 were waited for; matrix products, arithmetic and copies ran while one was open for 36% of the time, Pallas kernels for 0%

commit v1 on v0

v1 whole, which is shorter than its diff:
```python
import functools

import jax
import jax.numpy as jnp
from jax import lax
from jax.experimental import pallas as pl
from jax.experimental.pallas import tpu as pltpu
from jax.sharding import PartitionSpec as P

ITERS = 4
VERT_MIX = 0.2
COLUMN_DEPTH = 2.0
SPREAD_INV = 3.0
DRAFT_RATIO = 0.89
FREEZE_SALT = 0.0573
FREEZE_DEPTH = 0.76
THIN_RATE = 0.05
HEAT_SINK = 12.0
SALT_SINK = 6.0
VISC_FLOOR = 0.05
LANES = 128
MESH = pl.DeviceIdType.MESH
VMEM = pltpu.VMEM
SMEM = pltpu.SMEM
BIG = 58 * 1024 * 1024


def split(value):
    high = value.astype(jnp.bfloat16)
    return high, (value - high.astype(jnp.float32)).astype(jnp.bfloat16)


def turn_kernel(send_ref, tracers_ref, table_ref, picked_ref):
    levels, cells = tracers_ref.shape[1:]
    tile = 512

    @pl.loop(0, cells // tile)
    def _(step):
        at = pl.ds(pl.multiple_of(step * tile, tile), tile)
        for kind in range(2):
            block = tracers_ref[kind, :, at]
            block = jnp.concatenate(
                [block, jnp.zeros((LANES - levels, tile), jnp.float32)], axis=0
            )
            table_ref[kind, at, :] = block.T

    @pl.loop(0, send_ref.shape[0] // 16)
    def _(step):
        for inner in range(16):
            item = step * 16 + inner
            cell = send_ref[item]
            for kind in range(2):
                picked_ref[kind, pl.ds(item, 1), :] = table_ref[kind, pl.ds(cell, 1), :]


def mix_kernel(levels, nbr_ref, weight_ref, own_ref, table_ref, left_ref, right_ref,
               mixed_ref, extended, sem):
    step = pl.program_id(0)
    cells = table_ref.shape[1]
    rim = left_ref.shape[1]
    block = mixed_ref.shape[1]

    @pl.when(step == 0)
    def _():
        copies = [
            pltpu.make_async_copy(table_ref, extended.at[:, pl.ds(0, cells)], sem.at[0]),
            pltpu.make_async_copy(left_ref, extended.at[:, pl.ds(cells, rim)], sem.at[1]),
            pltpu.make_async_copy(right_ref, extended.at[:, pl.ds(cells + rim, rim)], sem.at[2]),
        ]
        for copy in copies:
            copy.start()
        for copy in copies:
            copy.wait()

    unroll = 8

    @pl.loop(0, block // unroll)
    def _(outer):
        base = outer * unroll
        for inner in range(unroll):
            cell = base + inner
            own = own_ref[0, cell]
            here = step * block + cell
            sums = [own * extended[kind, pl.ds(here, 1), :] for kind in range(2)]
            for k in range(nbr_ref.shape[0]):
                source = nbr_ref[k, cell]
                weight = weight_ref[k, cell]
                for kind in range(2):
                    sums[kind] = sums[kind] + weight * extended[kind, pl.ds(source, 1), :]
            for kind in range(2):
                mixed_ref[kind, pl.ds(cell, 1), :] = sums[kind]

    tile = 128
    lane = lax.broadcasted_iota(jnp.int32, (tile, LANES), 1)

    @pl.loop(0, block // tile)
    def _(part):
        first = pl.multiple_of(part * tile, tile)
        at = pl.ds(pl.multiple_of(step * block + first, tile), tile)
        for kind in range(2):
            column = extended[kind, at, :]
            above = jnp.where(lane == 0, column, pltpu.roll(column, 1, 1))
            below = jnp.where(lane == levels - 1, column, pltpu.roll(column, LANES - 1, 1))
            mixed_ref[kind, pl.ds(first, tile), :] += VERT_MIX * (above + below)


def melt_kernel(cell_ref, row_col_ref, row_lane_ref, col_ref, thick_ref, mixed_ref,
                ocean_ref, sums_ref, state, heat_cols, salt_cols, weighted, sem):
    levels, cells = ocean_ref.shape[1:]
    slots = heat_cols.shape[0]
    rows, width = thick_ref.shape
    copy = pltpu.make_async_copy(mixed_ref, state, sem)
    copy.start()
    copy.wait()

    @pl.loop(0, slots // 16)
    def _(step):
        for inner in range(16):
            slot = step * 16 + inner
            cell = cell_ref[slot]
            heat_cols[pl.ds(slot, 1), :] = state[0, pl.ds(cell, 1), :]
            salt_cols[pl.ds(slot, 1), :] = state[1, pl.ds(cell, 1), :]

    high, low = split(thick_ref[...])
    tile = 256
    sums_ref[...] = jnp.zeros_like(sums_ref)

    @pl.loop(0, slots // tile)
    def _(step):
        at = pl.ds(pl.multiple_of(step * tile, tile), tile)
        pick = (
            lax.broadcasted_iota(jnp.int32, (tile, rows), 1) == row_col_ref[at, :]
        ).astype(jnp.float32).astype(jnp.bfloat16)
        found = jnp.dot(pick, high, preferred_element_type=jnp.float32)
        found = found + jnp.dot(pick, low, preferred_element_type=jnp.float32)
        here = lax.broadcasted_iota(jnp.int32, (tile, width), 1) == col_ref[at, :]
        depth = DRAFT_RATIO * jnp.sum(jnp.where(here, found, 0.0), axis=1, keepdims=True)
        lane = lax.broadcasted_iota(jnp.int32, (tile, LANES), 1)
        center = (lane.astype(jnp.float32) + 0.5) * (COLUMN_DEPTH / levels)
        share = jnp.where(lane < levels, jnp.exp(-SPREAD_INV * (center - depth) ** 2), 0.0)
        share = share / jnp.sum(share, axis=1, keepdims=True)
        taken = share * (heat_cols[at, :] - FREEZE_SALT * salt_cols[at, :])
        melt = jnp.sum(taken, axis=1, keepdims=True) + FREEZE_DEPTH * depth
        weighted[at, :] = melt * share
        melt_high, melt_low = split(jnp.where(here, melt, 0.0))
        put = (
            lax.broadcasted_iota(jnp.int32, (rows, tile), 0) == row_lane_ref[:, at]
        ).astype(jnp.float32).astype(jnp.bfloat16)
        sums_ref[...] += jnp.dot(put, melt_high, preferred_element_type=jnp.float32) + jnp.dot(
            put, melt_low, preferred_element_type=jnp.float32
        )

    @pl.loop(0, slots // 16)
    def _(step):
        for inner in range(16):
            slot = step * 16 + inner
            cell = pl.ds(cell_ref[slot], 1)
            part = weighted[pl.ds(slot, 1), :]
            state[0, cell, :] = state[0, cell, :] - HEAT_SINK * part
            state[1, cell, :] = state[1, cell, :] - SALT_SINK * part

    span = 512

    @pl.loop(0, cells // span)
    def _(step):
        at = pl.ds(pl.multiple_of(step * span, span), span)
        for kind in range(2):
            ocean_ref[kind, :, at] = state[kind, at, :].T[:levels]


def ice_kernel(groups, domains, sums_ref, thick_ref, friction_ref, driving_ref, velocity_ref,
               ice_ref, out_ref, strip_in, strip, block_in, strips, diag, visc, iterate, resid, direct,
               send_a, recv_a, send_b, recv_b, send_c, recv_c, send_d, recv_d):
    g = lax.axis_index("grp")
    d = lax.axis_index("dom")
    rows, cols = thick_ref.shape
    tall = domains * rows
    height, width = friction_ref.shape

    barrier = pltpu.get_barrier_semaphore()
    for off in range(1, groups):
        pl.semaphore_signal(barrier, inc=1, device_id=((g + off) % groups, d), device_id_type=MESH)
    for off in range(1, domains):
        pl.semaphore_signal(barrier, inc=1, device_id=(g, (d + off) % domains), device_id_type=MESH)
    pl.semaphore_wait(barrier, groups + domains - 2)

    def strip_rows(which):
        return pl.ds(pl.multiple_of(which * tall, tall), tall)

    def block_rows(which):
        return pl.ds(pl.multiple_of(which * rows, rows), rows)

    def send(src, dst, sems, off, device):
        copy = pltpu.make_async_remote_copy(
            src_ref=src, dst_ref=dst, send_sem=sems[0].at[off - 1], recv_sem=sems[1].at[off - 1],
            device_id=device, device_id_type=MESH,
        )
        copy.start()
        return copy

    copies = []
    for off in range(1, groups):
        other = (g + off) % groups
        copies.append(send(sums_ref.at[strip_rows(other)], strip_in.at[off - 1],
                           (send_a, recv_a), off, (other, d)))
    total = sums_ref[strip_rows(g), :]
    for copy in copies:
        copy.wait()
    for off in range(1, groups):
        total = total + strip_in[off - 1]
    strip[...] = total

    copies = []
    for off in range(1, domains):
        other = (d + off) % domains
        copies.append(send(strip.at[block_rows(other)], block_in.at[off - 1],
                           (send_b, recv_b), off, (g, other)))
    melted = strip[block_rows(d), :]
    for copy in copies:
        copy.wait()
    for off in range(1, domains):
        melted = melted + block_in[off - 1]
    ice = thick_ref[...] - THIN_RATE * melted
    ice_ref[...] = ice
    strips[g, block_rows(d), :] = ice

    copies = []
    for off in range(1, domains):
        other = (d + off) % domains
        copies.append(send(strips.at[g, block_rows(d)], strips.at[g, block_rows(d)],
                           (send_c, recv_c), off, (g, other)))
    for copy in copies:
        copy.wait()
    copies = []
    for off in range(1, groups):
        other = (g + off) % groups
        copies.append(send(strips.at[g], strips.at[g], (send_d, recv_d), off, (other, d)))
    for copy in copies:
        copy.wait()

    thickness = jnp.concatenate([strips[i] for i in range(groups)], axis=1)
    row = lax.broadcasted_iota(jnp.int32, (height, width), 0)
    col = lax.broadcasted_iota(jnp.int32, (height, width), 1)

    def west(value):
        return jnp.where(col == 0, 0.0, pltpu.roll(value, 1, 1))

    def east(value):
        return jnp.where(col == width - 1, 0.0, pltpu.roll(value, width - 1, 1))

    def south(value):
        return jnp.where(row == 0, 0.0, pltpu.roll(value, 1, 0))

    def north(value):
        return jnp.where(row == height - 1, 0.0, pltpu.roll(value, height - 1, 0))

    visc[...] = VISC_FLOOR + 0.5 * thickness * thickness
    diag[...] = friction_ref[...] + 2.0 * visc[...] + west(visc[...]) + south(visc[...])

    def operate(value):
        viscosity = visc[...]
        image = friction_ref[...] * value + viscosity * (2.0 * value - east(value) - north(value))
        image = image + west(viscosity) * (value - west(value))
        return image + south(viscosity) * (value - south(value))

    iterate[...] = velocity_ref[...]
    resid[...] = driving_ref[...] * thickness - operate(velocity_ref[...])
    direct[...] = resid[...] / diag[...]
    norm = jnp.sum(resid[...] * direct[...], keepdims=True)

    def sweep(_, norm):
        direction = direct[...]
        image = operate(direction)
        length = norm / jnp.sum(direction * image, keepdims=True)
        iterate[...] += length * direction
        residual = resid[...] - length * image
        resid[...] = residual
        precond = residual / diag[...]
        following = jnp.sum(residual * precond, keepdims=True)
        direct[...] = precond + following / norm * direction
        return following

    lax.fori_loop(0, ITERS - 1, sweep, norm)
    direction = direct[...]
    image = operate(direction)
    last = jnp.sum(resid[...] * (resid[...] / diag[...]), keepdims=True)
    length = last / jnp.sum(direction * image, keepdims=True)
    iterate[...] += length * direction
    out_ref[...] = iterate[block_rows(d), pl.ds(pl.multiple_of(g * cols, cols), cols)]


def local(tracers, mix_weights, neighbors, send_list, slot_cell, slot_owner, slot_node,
          thickness, friction, driving, velocity):
    levels, cells = tracers.shape[1:]
    groups = lax.axis_size("grp")
    domains = lax.axis_size("dom")
    devices = groups * domains
    slots = slot_cell.shape[0]
    rim = send_list.shape[0] // 2
    rows, cols = thickness.shape
    f32 = jnp.float32
    whole = pl.BlockSpec(memory_space=VMEM)
    scalars = pl.BlockSpec(memory_space=SMEM)
    anywhere = pl.BlockSpec(memory_space=pl.ANY)
    big = pltpu.CompilerParams(vmem_limit_bytes=BIG)

    shards = lax.all_gather(
        jnp.concatenate([thickness, friction, driving, velocity], axis=0), ("grp", "dom"), axis=0
    ).reshape(devices, 4, rows, cols)
    thick_table = shards[:, 0].reshape(devices * rows, cols)
    grids = [
        shards[:, i].reshape(groups, domains * rows, cols).transpose(1, 0, 2).reshape(
            domains * rows, groups * cols)
        for i in range(1, 4)
    ]

    table, picked = pl.pallas_call(
        turn_kernel,
        out_shape=(jax.ShapeDtypeStruct((2, cells, LANES), f32),
                   jax.ShapeDtypeStruct((2, 2 * rim, LANES), f32)),
        in_specs=[scalars, whole],
        out_specs=(whole, whole),
        compiler_params=big,
    )(send_list, tracers)
    forward = [(i, (i + 1) % domains) for i in range(domains)]
    backward = [(target, source) for source, target in forward]
    left = lax.ppermute(picked[:, rim:], "dom", forward)
    right = lax.ppermute(picked[:, :rim], "dom", backward)

    own_weight = (1.0 - 2.0 * VERT_MIX) - jnp.sum(mix_weights, axis=0, keepdims=True)
    block = 1024
    count = neighbors.shape[0]
    mixed = pl.pallas_call(
        functools.partial(mix_kernel, levels),
        grid=(cells // block,),
        out_shape=jax.ShapeDtypeStruct((2, cells, LANES), f32),
        in_specs=[
            pl.BlockSpec((count, block), lambda i: (0, i), memory_space=SMEM),
            pl.BlockSpec((count, block), lambda i: (0, i), memory_space=SMEM),
            pl.BlockSpec((1, block), lambda i: (0, i), memory_space=SMEM),
            anywhere, anywhere, anywhere,
        ],
        out_specs=pl.BlockSpec((2, block, LANES), lambda i: (0, i, 0)),
        scratch_shapes=[pltpu.VMEM((2, cells + 2 * rim, LANES), f32), pltpu.SemaphoreType.DMA((3,))],
        compiler_params=big,
        cost_estimate=pl.CostEstimate(flops=200_000_000, bytes_accessed=200_000_000, transcendentals=0),
    )(neighbors, mix_weights, own_weight, table, left, right)

    grid_row = slot_owner[:, 0] * rows + slot_node // cols
    grid_col = slot_node % cols
    ocean, sums = pl.pallas_call(
        melt_kernel,
        out_shape=(jax.ShapeDtypeStruct((2, levels, cells), f32),
                   jax.ShapeDtypeStruct((devices * rows, cols), f32)),
        in_specs=[scalars, whole, whole, whole, whole, anywhere],
        out_specs=(whole, whole),
        scratch_shapes=[
            pltpu.VMEM((2, cells, LANES), f32),
            pltpu.VMEM((slots, LANES), f32),
            pltpu.VMEM((slots, LANES), f32),
            pltpu.VMEM((slots, LANES), f32),
            pltpu.SemaphoreType.DMA,
        ],
        compiler_params=big,
    )(slot_cell, grid_row[:, None], grid_row[None, :], grid_col[:, None], thick_table, mixed)

    grid_shape = (domains * rows, groups * cols)
    dma = pltpu.SemaphoreType.DMA
    ice, iterate = pl.pallas_call(
        functools.partial(ice_kernel, groups, domains),
        out_shape=(jax.ShapeDtypeStruct((rows, cols), f32),) * 2,
        in_specs=[whole] * 5,
        out_specs=(whole, whole),
        scratch_shapes=[
            pltpu.VMEM((groups - 1, domains * rows, cols), f32),
            pltpu.VMEM((domains * rows, cols), f32),
            pltpu.VMEM((domains - 1, rows, cols), f32),
            pltpu.VMEM((groups, domains * rows, cols), f32),
        ] + [pltpu.VMEM(grid_shape, f32)] * 5 + [
            dma((groups - 1,)), dma((groups - 1,)), dma((domains - 1,)), dma((domains - 1,)),
            dma((domains - 1,)), dma((domains - 1,)), dma((groups - 1,)), dma((groups - 1,)),
        ],
        compiler_params=pltpu.CompilerParams(
            collective_id=0, has_side_effects=True, vmem_limit_bytes=BIG
        ),
    )(sums, thickness, *grids)
    return ocean, ice, iterate


def solution(mesh):
    return jax.shard_map(
        local,
        mesh=mesh,
        in_specs=(
            P(None, None, ("grp", "dom")),
            P(None, ("grp", "dom")),
            P(None, ("grp", "dom")),
            P(("grp", "dom")),
            P(("grp", "dom")),
            P(("grp", "dom"), None),
            P(("grp", "dom")),
            P("dom", "grp"),
            P("dom", "grp"),
            P("dom", "grp"),
            P("dom", "grp"),
        ),
        out_specs=(P(None, None, ("grp", "dom")), P("dom", "grp"), P("dom", "grp")),
        check_vma=False,
    )
```

time: 1120 us -> 251 us (0.22)
  local copies, waits for them, and re-layouts: 405 us -> 14.2 us
  other arithmetic: 284 us -> 2.11 us
  blocking collectives: 280 us -> 0 us
  Pallas kernels: 0 us -> 174 us
  starting transfers between devices: 75.1 us -> 5.14 us
  waiting for transfers between devices: 62.9 us -> 40.7 us
    gather x18 -> x0, local copies, waits for them, and re-layouts: 332 us -> none  [the longest x12 262 us: local(): gathered = jnp.take(extended, neighbors[neighbor], axis=1)]
    psum x7 -> x0, blocking collectives: 280 us -> none  [the longest x3 120 us: local(): curvature_sum = lax.psum(jnp.sum(direction * image), ('grp', 'dom'))]
    scatter-add x2 -> x0, other arithmetic: 220 us -> none  [the longest x1 194 us: local(): ocean_out = mixed_state.at[:, :, slot_cell].add(increments)]
    pallas_call x0 -> x4, Pallas kernels: none -> 174 us  [the longest x1 96.7 us: local(): pl.pallas_call(functools.partial(mix_kernel, levels), grid=(cells // bloc...]
    ppermute x22 -> x2, starting transfers between devices: 56.9 us -> 5.1 us  [the longest x1 3.03 us: local(): right = lax.ppermute(picked[:, :rim], 'dom', backward)]
    all_to_all x4 -> x0, waiting for transfers between devices: 35.6 us -> none  [the longest x1 35.6 us: local(): lax.all_to_all(packed, ('grp', 'dom'), split_axis=1, concat_axis=1, tiled...]
    add x7 -> x0, other arithmetic: 21.9 us -> none  [the longest x1 14.2 us: local(): horizontal + mix_weights[neighbor][None, :] * (gathered - flat_tracers)]
    scatter x2 -> x0, local copies, waits for them, and re-layouts: 20.2 us -> none  [the longest x1 11.4 us: local(): packed = jnp.zeros((2 * levels, devices * capacity), jnp.float32).at[:, t...]
  transfers between devices with their start and end apart: 26 -> 3, of which waited for: 10 -> 2; matrix products, arithmetic and copies ran while one was open for 36% -> 2% of each run, Pallas kernels for 0% -> 44%
where the time goes in v1:
time: 251 us; the launch traced here: 250 us
  Pallas kernels  174 us (69%)
  waiting for transfers between devices  40.7 us (16%)
  local copies, waits for them, and re-layouts  14.2 us (6%)
  between operations  14.1 us (6%)
  starting transfers between devices  5.14 us (2%)
    pallas_call x1, Pallas kernels, local(): pl.pallas_call(functools.partial(mix_kernel, levels), grid=(cells // bloc...  96.7 us
    ppermute x1, waiting for transfers between devices, local(): left = lax.ppermute(picked[:, rim:], 'dom', forward)  39.1 us
    pallas_call x1, Pallas kernels, local(): pl.pallas_call(functools.partial(ice_kernel, groups, domains), out_shape=...  35.5 us
    pallas_call x1, Pallas kernels, local(): pl.pallas_call(melt_kernel, out_shape=(jax.ShapeDtypeStruct((2, levels, c...  29.2 us
    pallas_call x1, Pallas kernels, local(): pl.pallas_call(turn_kernel, out_shape=(jax.ShapeDtypeStruct((2, cells, LA...  12.7 us
  transfers between devices with their start and end apart: 3, of which 2 were waited for; matrix products, arithmetic and copies ran while one was open for 2% of the time, Pallas kernels for 44%

profile of v1, /device:TPU:1, one launch (start us, length us, event | category | flops | bytes accessed | tf_op | source)
XLA Modules:
  0.0 250.3 jit_solution(16356485417836720065)
XLA Ops:
  7.2 0.0 all-gather.3.cloned.1.call-start
  7.2 1.4 pad_maximum_fusion
  8.6 0.0 all-gather.3.cloned.1.call-update
  8.7 12.7 %shard_map.130 = (f32[2,8192,128]{2,1,0:T(8,128)}, f32[2,2048,128]{2,1,0:T(8,128)}) custom-call(s32[2048]{0:T(1024)} %send_ref.1, f32[2,80,8192]{2,1,0:T(8,128)} %tracers_ref.1), custom_call_target="tpu_custom_call" | custom-call | tf_op jit(solution)/shard_map/pallas_call | solution.py:317
  21.4 2.7 %fusion.4 = (f32[2,1024,128]{2,1,0:T(8,128)S(1)}, f32[2,1024,128]{2,1,0:T(8,128)}) fusion(f32[2,2048,128]{2,1,0:T(8,128)} %get-tuple-element.10), kind=kLoop, calls=%fused_computation.13 | loop fusion | bytes 4194304 | tf_op jit(solution)/shard_map/slice | solution.py:328
  24.1 2.1 collective-permute-start
  26.2 3.0 %collective-permute-start.1 = (f32[2,1024,128]{2,1,0:T(8,128)S(1)}, f32[2,1024,128]{2,1,0:T(8,128)S(1)}, u32[]{:S(2)}, u32[]{:S(2)}) collective-permute-start(f32[2,1024,128]{2,1,0:T(8,128)S(1)} %get-tuple-element.19), channel_id=1, source_target_pairs={{1,0},{2,1},{3,2},{4,3},{5,4},{6,5},{7,6},{0,7},{9,8},{10,9},{11,1... | collective-permute-start | bytes 3145736 | tf_op jit(solution)/shard_map/ppermute | solution.py:328
  29.3 1.4 copy.20.row_col_ref
  30.6 1.4 copy.21.col_ref
  32.0 0.1 reduce_sum.9
  32.1 0.6 broadcast_subtract_fusion
  32.7 39.1 %collective-permute-done.left_ref = f32[2,1024,128]{2,1,0:T(8,128)S(1)} collective-permute-done((f32[2,1024,128]{2,1,0:T(8,128)}, f32[2,1024,128]{2,1,0:T(8,128)S(1)}, u32[]{:S(2)}, u32[]{:S(2)}) %collective-permute-start) | collective-permute-done | bytes 1048608 | tf_op jit(solution)/shard_map/ppermute | solution.py:327
  71.8 1.6 collective-permute-done.1.right_ref
  73.3 1.0 copy-done.2
  74.3 96.7 %shard_map.131.mixed_ref = f32[2,8192,128]{2,1,0:T(8,128)} custom-call(s32[6,8192]{1,0:T(8,128)} %nbr_ref.1, f32[6,8192]{1,0:T(8,128)} %weight_ref.1, f32[1,8192]{1,0:T(1,128)} %bitcast.30, f32[2,8192,128]{2,1,0:T(8,128)} %get-tuple-element.9.table_ref, f32[2,1024,128]{2,1,0:T(8,128)} %copy-done.1, f32[2,1024,128]{2,1,0:T(8,128)} %copy-done.2), custom_call_target="tpu_custom_call" | custom-call | flops 200000000 | bytes 200000000 | tf_op jit(solution)/shard_map/pallas_call | solution.py:333
  171.1 0.0 all-gather.3.cloned.1.call-done
  171.1 2.5 %fusion.3 = (f32[32,1,16,256]{3,2,1,0:T(8,128)S(1)}, f32[32,1,16,256]{3,2,1,0:T(8,128)S(1)}, f32[32,1,16,256]{3,2,1,0:T(8,128)S(1)}, f32[32,1,16,256]{3,2,1,0:T(8,128)}) fusion(f32[32,4,16,256]{3,2,1,0:T(8,128)} %bitcast.22), kind=kLoop, calls=%fused_computation.12 | loop fusion | bytes 4194304 | tf_op jit(solution)/shard_map/slice | solution.py:312
  173.6 0.9 copy.25
  174.5 0.9 copy.26
  175.3 0.8 copy.27
  176.2 29.2 %shard_map.132 = (f32[2,80,8192]{2,1,0:T(8,128)}, f32[512,256]{1,0:T(8,128)}) custom-call(s32[2048]{0:T(1024)} %cell_ref.1, s32[2048,1]{1,0:T(8,128)} %copy.20.row_col_ref, s32[1,2048]{1,0:T(1,128)} %bitcast.32, s32[2048,1]{1,0:T(8,128)} %copy.21.col_ref, f32[512,256]{1,0:T(8,128)} %bitcast.29, f32[2,8192,128]{2,1,0:T(8,128)} %shard_map.131.mixed_ref), custom_call_target="tpu_custom_call" | custom-call | tf_op jit(solution)/shard_map/pallas_call | solution.py:351
  205.4 35.5 %shard_map.133 = (f32[16,256]{1,0:T(8,128)}, f32[16,256]{1,0:T(8,128)}) custom-call(f32[512,256]{1,0:T(8,128)} %get-tuple-element.12.sums_ref, f32[16,256]{1,0:T(8,128)} %thick_ref.1, f32[128,1024]{1,0:T(8,128)} %bitcast.23, f32[128,1024]{1,0:T(8,128)} %bitcast.24, f32[128,1024]{1,0:T(8,128)} %bitcast.25), custom_call_target="tpu_custom_call" | custom-call | tf_op jit(solution)/shard_map/pallas_call | solution.py:369
  240.8 1.3 copy.30
  242.2 1.3 copy.31
  (13 shorter events, 0.0 us)
Async XLA Ops:
  7.2 22.0 %copy-start.4 = (s32[2048,1]{0,1:T(1,128)S(1)}, s32[2048,1]{0,1:T(1,128)}, u32[]{:S(2)}) copy-start(s32[2048,1]{0,1:T(1,128)} %param.16) | copy-start | bytes 24580
  7.2 22.0 %copy-start.5 = (s32[2048]{0:T(1024)S(1)}, s32[2048]{0:T(1024)}, u32[]{:S(2)}) copy-start(s32[2048]{0:T(1024)} %param.17) | copy-start | bytes 24580
  7.2 163.9 %all-gather.3.cloned.1.call-start = ((), (), s32[]{:S(2)}) async-start(), calls=%async_computation | async-start | bytes 2162688 | tf_op jit(solution)/shard_map/all_gather | solution.py:307
  8.6 23.3 %copy-start = (f32[6,8192]{1,0:T(8,128)S(1)}, f32[6,8192]{1,0:T(8,128)}, u32[]{:S(2)}) copy-start(f32[6,8192]{1,0:T(8,128)} %weight_ref.1) | copy-start | bytes 589828
  24.1 47.7 %collective-permute-start = (f32[2,1024,128]{2,1,0:T(8,128)}, f32[2,1024,128]{2,1,0:T(8,128)S(1)}, u32[]{:S(2)}, u32[]{:S(2)}) collective-permute-start(f32[2,1024,128]{2,1,0:T(8,128)} %get-tuple-element.20), channel_id=1, source_target_pairs={{0,1},{1,2},{2,3},{3,4},{4,5},{5,6},{6,7},{7,0},{8,9},{9,10},{10,1... | collective-permute-start | bytes 3145736 | tf_op jit(solution)/shard_map/ppermute | solution.py:327
  26.2 47.2 %collective-permute-start.1 = (f32[2,1024,128]{2,1,0:T(8,128)S(1)}, f32[2,1024,128]{2,1,0:T(8,128)S(1)}, u32[]{:S(2)}, u32[]{:S(2)}) collective-permute-start(f32[2,1024,128]{2,1,0:T(8,128)S(1)} %get-tuple-element.19), channel_id=1, source_target_pairs={{1,0},{2,1},{3,2},{4,3},{5,4},{6,5},{7,6},{0,7},{9,8},{10,9},{11,1... | collective-permute-start | bytes 3145736 | tf_op jit(solution)/shard_map/ppermute | solution.py:328
  29.2 141.8 %copy-start.3 = (s32[2048]{0:T(1024)}, s32[2048]{0:T(1024)S(1)}, u32[]{:S(2)}) copy-start(s32[2048]{0:T(1024)S(1)} %get-tuple-element.22) | copy-start | bytes 24580
  71.7 1.6 copy-start.1
  73.3 1.0 copy-start.2
Sparse Core Ops, SparseCore 0:
  11.0 79.3 all-gather.2

commit v2 on v1

--- a/solution.py
+++ b/solution.py
@@ -22,6 +22,8 @@
 MESH = pl.DeviceIdType.MESH
 VMEM = pltpu.VMEM
 SMEM = pltpu.SMEM
+LEAD = 2
+GROUP = 32
 BIG = 58 * 1024 * 1024
 
 
@@ -30,78 +32,105 @@
     return high, (value - high.astype(jnp.float32)).astype(jnp.bfloat16)
 
 
-def turn_kernel(send_ref, tracers_ref, table_ref, picked_ref):
+def columns_of(block):
+    pad = jnp.zeros((LANES - block.shape[0], block.shape[1]), jnp.float32)
+    return jnp.concatenate([block, pad], axis=0).T
+
+
+def turn_kernel(send_ref, tracers_ref, table_ref, first_ref, second_ref, picked):
     levels, cells = tracers_ref.shape[1:]
+    rim = first_ref.shape[2]
     tile = 512
 
     @pl.loop(0, cells // tile)
     def _(step):
         at = pl.ds(pl.multiple_of(step * tile, tile), tile)
         for kind in range(2):
-            block = tracers_ref[kind, :, at]
-            block = jnp.concatenate(
-                [block, jnp.zeros((LANES - levels, tile), jnp.float32)], axis=0
-            )
-            table_ref[kind, at, :] = block.T
-
-    @pl.loop(0, send_ref.shape[0] // 16)
-    def _(step):
-        for inner in range(16):
-            item = step * 16 + inner
+            table_ref[kind, at, :] = columns_of(tracers_ref[kind, :, at])
+
+    @pl.loop(0, send_ref.shape[0] // 32)
+    def _(step):
+        for inner in range(32):
+            item = step * 32 + inner
             cell = send_ref[item]
             for kind in range(2):
-                picked_ref[kind, pl.ds(item, 1), :] = table_ref[kind, pl.ds(cell, 1), :]
-
-
-def mix_kernel(levels, nbr_ref, weight_ref, own_ref, table_ref, left_ref, right_ref,
-               mixed_ref, extended, sem):
+                picked[kind, pl.ds(item, 1), :] = table_ref[kind, pl.ds(cell, 1), :]
+
+    for half, out_ref in enumerate((first_ref, second_ref)):
+        for start in range(0, rim, tile):
+            for kind in range(2):
+                rows = picked[kind, half * rim + start : half * rim + start + tile, :]
+                out_ref[kind, :, start : start + tile] = rows.T[:levels]
+
+
+def add_columns(nbr_ref, weight_ref, table, mixed_ref, first, unroll):
+    for inner in range(unroll):
+        cell = first + inner
+        sums = [mixed_ref[kind, pl.ds(cell, 1), :] for kind in range(2)]
+        for k in range(nbr_ref.shape[0]):
+            source = nbr_ref[k, cell]
+            weight = weight_ref[k, cell]
+            for kind in range(2):
+                sums[kind] = sums[kind] + weight * table[kind, pl.ds(source, 1), :]
+        for kind in range(2):
+            mixed_ref[kind, pl.ds(cell, 1), :] = sums[kind]
+
+
+def near_kernel(nbr_ref, weight_ref, own_ref, tracers_ref, table_ref, mixed_ref, table, sem):
+    block = mixed_ref.shape[1]
+
+    @pl.when(pl.program_id(0) == 0)
+    def _():
+        copy = pltpu.make_async_copy(table_ref, table, sem)
+        copy.start()
+        copy.wait()
+
+    tile = 512
+    for start in range(0, block, tile):
+        for kind in range(2):
+            here = tracers_ref[kind, :, start : start + tile]
+            above = jnp.concatenate([here[:1], here[:-1]], axis=0)
+            below = jnp.concatenate([here[1:], here[-1:]], axis=0)
+            value = own_ref[:, start : start + tile] * here + VERT_MIX * (above + below)
+            mixed_ref[kind, start : start + tile, :] = columns_of(value)
+
+    @pl.loop(0, block // GROUP)
+    def _(outer):
+        add_columns(nbr_ref, weight_ref, table, mixed_ref, outer * GROUP, GROUP)
+
+
+def far_kernel(flag_ref, nbr_ref, weight_ref, lead_nbr_ref, lead_weight_ref, table_ref, left_ref, right_ref,
+               near_ref, mixed_ref, extended, sem):
     step = pl.program_id(0)
     cells = table_ref.shape[1]
-    rim = left_ref.shape[1]
+    rim = left_ref.shape[2]
     block = mixed_ref.shape[1]
+    tile = 512
 
     @pl.when(step == 0)
     def _():
-        copies = [
-            pltpu.make_async_copy(table_ref, extended.at[:, pl.ds(0, cells)], sem.at[0]),
-            pltpu.make_async_copy(left_ref, extended.at[:, pl.ds(cells, rim)], sem.at[1]),
-            pltpu.make_async_copy(right_ref, extended.at[:, pl.ds(cells + rim, rim)], sem.at[2]),
-        ]
-        for copy in copies:
-            copy.start()
-        for copy in copies:
-            copy.wait()
-
-    unroll = 8
-
-    @pl.loop(0, block // unroll)
+        copy = pltpu.make_async_copy(table_ref, extended.at[:, pl.ds(0, cells)], sem)
+        copy.start()
+        for side, ref in enumerate((left_ref, right_ref)):
+            for start in range(0, rim, tile):
+                for kind in range(2):
+                    first = cells + side * rim + start
+                    extended[kind, first : first + tile, :] = columns_of(ref[kind, :, start : start + tile])
+        copy.wait()
+
+    for kind in range(2):
+        mixed_ref[kind] = near_ref[kind]
+
+    @pl.loop(0, block // GROUP)
     def _(outer):
-        base = outer * unroll
-        for inner in range(unroll):
-            cell = base + inner
-            own = own_ref[0, cell]
-            here = step * block + cell
-            sums = [own * extended[kind, pl.ds(here, 1), :] for kind in range(2)]
-            for k in range(nbr_ref.shape[0]):
-                source = nbr_ref[k, cell]
-                weight = weight_ref[k, cell]
-                for kind in range(2):
-                    sums[kind] = sums[kind] + weight * extended[kind, pl.ds(source, 1), :]
-            for kind in range(2):
-                mixed_ref[kind, pl.ds(cell, 1), :] = sums[kind]
-
-    tile = 128
-    lane = lax.broadcasted_iota(jnp.int32, (tile, LANES), 1)
-
-    @pl.loop(0, block // tile)
-    def _(part):
-        first = pl.multiple_of(part * tile, tile)
-        at = pl.ds(pl.multiple_of(step * block + first, tile), tile)
-        for kind in range(2):
-            column = extended[kind, at, :]
-            above = jnp.where(lane == 0, column, pltpu.roll(column, 1, 1))
-            below = jnp.where(lane == levels - 1, column, pltpu.roll(column, LANES - 1, 1))
-            mixed_ref[kind, pl.ds(first, tile), :] += VERT_MIX * (above + below)
+        first = outer * GROUP
+        add_columns(nbr_ref, weight_ref, extended, mixed_ref, first, GROUP)
+
+        @pl.when(flag_ref[step * (block // GROUP) + outer] > 0)
+        def _():
+            @pl.loop(0, GROUP)
+            def _(inner):
+                add_columns(lead_nbr_ref, lead_weight_ref, extended, mixed_ref, first + inner, 1)
 
 
 def melt_kernel(cell_ref, row_col_ref, row_lane_ref, col_ref, thick_ref, mixed_ref,
@@ -113,10 +142,10 @@
     copy.start()
     copy.wait()
 
-    @pl.loop(0, slots // 16)
-    def _(step):
-        for inner in range(16):
-            slot = step * 16 + inner
+    @pl.loop(0, slots // 32)
+    def _(step):
+        for inner in range(32):
+            slot = step * 32 + inner
             cell = cell_ref[slot]
             heat_cols[pl.ds(slot, 1), :] = state[0, pl.ds(cell, 1), :]
             salt_cols[pl.ds(slot, 1), :] = state[1, pl.ds(cell, 1), :]
@@ -156,8 +185,10 @@
             slot = step * 16 + inner
             cell = pl.ds(cell_ref[slot], 1)
             part = weighted[pl.ds(slot, 1), :]
-            state[0, cell, :] = state[0, cell, :] - HEAT_SINK * part
-            state[1, cell, :] = state[1, cell, :] - SALT_SINK * part
+            heat = state[0, cell, :] - HEAT_SINK * part
+            salt = state[1, cell, :] - SALT_SINK * part
+            state[0, cell, :] = heat
+            state[1, cell, :] = salt
 
     span = 512
 
@@ -314,37 +345,74 @@
         for i in range(1, 4)
     ]
 
-    table, picked = pl.pallas_call(
+    halo = jax.ShapeDtypeStruct((2, levels, rim), f32)
+    table, to_left, to_right = pl.pallas_call(
         turn_kernel,
-        out_shape=(jax.ShapeDtypeStruct((2, cells, LANES), f32),
-                   jax.ShapeDtypeStruct((2, 2 * rim, LANES), f32)),
+        out_shape=(jax.ShapeDtypeStruct((2, cells, LANES), f32), halo, halo),
         in_specs=[scalars, whole],
-        out_specs=(whole, whole),
+        out_specs=(whole, whole, whole),
+        scratch_shapes=[pltpu.VMEM((2, 2 * rim, LANES), f32)],
         compiler_params=big,
     )(send_list, tracers)
     forward = [(i, (i + 1) % domains) for i in range(domains)]
     backward = [(target, source) for source, target in forward]
-    left = lax.ppermute(picked[:, rim:], "dom", forward)
-    right = lax.ppermute(picked[:, :rim], "dom", backward)
+    left = lax.ppermute(to_right, "dom", forward)
+    right = lax.ppermute(to_left, "dom", backward)
+
+    count = neighbors.shape[0]
+    index = [neighbors[k] for k in range(count)]
+    weight = [mix_weights[k] for k in range(count)]
+    for place in range(LEAD):
+        for k in range(count - 1, place, -1):
+            swap = index[k] < index[k - 1]
+            index[k - 1], index[k] = (
+                jnp.where(swap, index[k], index[k - 1]), jnp.where(swap, index[k - 1], index[k]))
+            weight[k - 1], weight[k] = (
+                jnp.where(swap, weight[k], weight[k - 1]), jnp.where(swap, weight[k - 1], weight[k]))
+    lead_index, lead_weight = jnp.stack(index[:LEAD]), jnp.stack(weight[:LEAD])
+    rest_index, rest_weight = jnp.stack(index[LEAD:]), jnp.stack(weight[LEAD:])
+    inside = lead_index < cells
+    near_index = jnp.where(inside, lead_index, 0)
+    near_weight = jnp.where(inside, lead_weight, 0.0)
+    far_weight = jnp.where(inside, 0.0, lead_weight)
+    flags = jnp.any(jnp.logical_not(inside).reshape(LEAD, cells // GROUP, GROUP), axis=(0, 2)).astype(jnp.int32)
 
     own_weight = (1.0 - 2.0 * VERT_MIX) - jnp.sum(mix_weights, axis=0, keepdims=True)
     block = 1024
-    count = neighbors.shape[0]
-    mixed = pl.pallas_call(
-        functools.partial(mix_kernel, levels),
+
+    def listed(number):
+        return pl.BlockSpec((number, block), lambda i: (0, i), memory_space=SMEM)
+
+    columns = pl.BlockSpec((2, block, LANES), lambda i: (0, i, 0))
+    near = pl.pallas_call(
+        near_kernel,
         grid=(cells // block,),
         out_shape=jax.ShapeDtypeStruct((2, cells, LANES), f32),
         in_specs=[
-            pl.BlockSpec((count, block), lambda i: (0, i), memory_space=SMEM),
-            pl.BlockSpec((count, block), lambda i: (0, i), memory_space=SMEM),
-            pl.BlockSpec((1, block), lambda i: (0, i), memory_space=SMEM),
-            anywhere, anywhere, anywhere,
+            listed(LEAD), listed(LEAD),
+            pl.BlockSpec((1, block), lambda i: (0, i)),
+            pl.BlockSpec((2, levels, block), lambda i: (0, 0, i)),
+            anywhere,
         ],
-        out_specs=pl.BlockSpec((2, block, LANES), lambda i: (0, i, 0)),
-        scratch_shapes=[pltpu.VMEM((2, cells + 2 * rim, LANES), f32), pltpu.SemaphoreType.DMA((3,))],
+        out_specs=columns,
+        scratch_shapes=[pltpu.VMEM((2, cells, LANES), f32), pltpu.SemaphoreType.DMA],
+        compiler_params=big,
+        cost_estimate=pl.CostEstimate(flops=100_000_000, bytes_accessed=130_000_000, transcendentals=0),
+    )(near_index, near_weight, own_weight, tracers, table)
+    edge = pl.BlockSpec((2, levels, rim), lambda i: (0, 0, 0))
+    mixed = pl.pallas_call(
+        far_kernel,
+        grid=(cells // block,),
+        out_shape=jax.ShapeDtypeStruct((2, cells, LANES), f32),
+        in_specs=[
+            scalars, listed(count - LEAD), listed(count - LEAD), listed(LEAD), listed(LEAD),
+            anywhere, edge, edge, columns,
+        ],
+        out_specs=columns,
+        scratch_shapes=[pltpu.VMEM((2, cells + 2 * rim, LANES), f32), pltpu.SemaphoreType.DMA],
         compiler_params=big,
         cost_estimate=pl.CostEstimate(flops=200_000_000, bytes_accessed=200_000_000, transcendentals=0),
-    )(neighbors, mix_weights, own_weight, table, left, right)
+    )(flags, rest_index, rest_weight, lead_index, far_weight, table, left, right, near)
 
     grid_row = slot_owner[:, 0] * rows + slot_node // cols
     grid_col = slot_node % cols

time: 251 us -> 217 us (0.86)
  waiting for transfers between devices: 40.7 us -> 0.04 us
  Pallas kernels: 174 us -> 179 us
  other arithmetic: 2.11 us -> 7.1 us
    ppermute x2, waiting for transfers between devices: 40.6 us -> 0.01 us  [the longest x1 0.01 us: local(): left = lax.ppermute(to_right, 'dom', forward)]
    pallas_call x1 -> x2, Pallas kernels: 96.7 us -> 102 us  [the longest x1 63.5 us: local(): pl.pallas_call(far_kernel, grid=(cells // block,), out_shape=jax.ShapeDty...]
    select_n x0 -> x9, other arithmetic: none -> 3.6 us  [the longest x2 0.87 us: local(): jnp.where(swap, weight[k], weight[k - 1])]
    slice x1 -> x0, local copies, waits for them, and re-layouts: 2.7 us -> none  [local(): right = lax.ppermute(picked[:, :rim], 'dom', backward)]
  transfers between devices with their start and end apart: 3 -> 3, of which waited for: 2 -> 0; matrix products, arithmetic and copies ran while one was open for 2% -> 5% of each run, Pallas kernels for 44% -> 47%
where the time goes in v2:
time: 217 us; the launch traced here: 218 us
  Pallas kernels  179 us (82%)
  between operations  14.3 us (7%)
  local copies, waits for them, and re-layouts  12.4 us (6%)
  other arithmetic  7.1 us (3%)
  starting transfers between devices  5.15 us (2%)
    pallas_call x1, Pallas kernels, local(): pl.pallas_call(far_kernel, grid=(cells // block,), out_shape=jax.ShapeDty...  63.5 us
    pallas_call x1, Pallas kernels, local(): pl.pallas_call(near_kernel, grid=(cells // block,), out_shape=jax.ShapeDt...  38.4 us
    pallas_call x1, Pallas kernels, local(): pl.pallas_call(functools.partial(ice_kernel, groups, domains), out_shape=...  35.8 us
    pallas_call x1, Pallas kernels, local(): pl.pallas_call(melt_kernel, out_shape=(jax.ShapeDtypeStruct((2, levels, c...  28.9 us
    pallas_call x1, Pallas kernels, local(): pl.pallas_call(turn_kernel, out_shape=(jax.ShapeDtypeStruct((2, cells, LA...  12.2 us
  transfers between devices with their start and end apart: 3, of which 0 were waited for; matrix products, arithmetic and copies ran while one was open for 5% of the time, Pallas kernels for 47%

profile of v2, /device:TPU:1, one launch (start us, length us, event | category | flops | bytes accessed | tf_op | source)
XLA Modules:
  0.0 217.8 jit_solution(9547324350119138647)
XLA Ops:
  7.3 12.2 %shard_map.130 = (f32[2,8192,128]{2,1,0:T(8,128)}, f32[2,80,1024]{2,1,0:T(8,128)}, f32[2,80,1024]{2,1,0:T(8,128)}) custom-call(s32[2048]{0:T(1024)} %send_ref.1, f32[2,80,8192]{2,1,0:T(8,128)} %tracers_ref.3), custom_call_target="tpu_custom_call" | custom-call | tf_op jit(solution)/shard_map/pallas_call | solution.py:349
  19.5 2.1 collective-permute-start
  21.6 3.0 %collective-permute-start.1 = (f32[2,80,1024]{2,1,0:T(8,128)}, f32[2,80,1024]{2,1,0:T(8,128)S(1)}, u32[]{:S(2)}, u32[]{:S(2)}) collective-permute-start(f32[2,80,1024]{2,1,0:T(8,128)} %get-tuple-element.12), channel_id=1, source_target_pairs={{1,0},{2,1},{3,2},{4,3},{5,4},{6,5},{7,6},{0,7},{9,8},{10,9},{11,1... | collective-permute-start | bytes 1966088 | tf_op jit(solution)/shard_map/ppermute | solution.py:360
  24.6 0.6 pad_maximum_fusion.1
  25.7 0.6 broadcast_subtract_fusion
  27.4 0.9 fusion.5
  28.6 0.6 convert_element_type.3.flag_ref
  29.3 1.4 copy.27.row_col_ref
  30.6 1.4 copy.28.col_ref
  32.0 0.7 broadcast_select_fusion
  32.7 0.8 broadcast_select_fusion.1
  33.5 38.4 %shard_map.131.near_ref = f32[2,8192,128]{2,1,0:T(8,128)} custom-call(s32[2,8192]{1,0:T(2,128)} %get-tuple-element.53.nbr_ref, f32[2,8192]{1,0:T(2,128)} %get-tuple-element.51.weight_ref, f32[1,8192]{1,0:T(1,128)} %bitcast.30, f32[2,80,8192]{2,1,0:T(8,128)} %tracers_ref.3, f32[2,8192,128]{2,1,0:T(8,128)} %get-tuple-element.10.table_ref), custom_call_target="tpu_custom_call" | custom-call | flops 100000000 | bytes 130000000 | tf_op jit(solution)/shard_map/pallas_call | solution.py:387
  72.2 0.8 pad_maximum_fusion.weight_ref
  73.1 0.8 pad_add_fusion.nbr_ref
  73.9 0.9 copy-done.2
  74.9 63.5 %shard_map.132.mixed_ref = f32[2,8192,128]{2,1,0:T(8,128)} custom-call(s32[256]{0:T(256)} %convert_element_type.3.flag_ref, s32[4,8192]{1,0:T(4,128)} %pad_add_fusion.nbr_ref, f32[4,8192]{1,0:T(4,128)} %pad_maximum_fusion.weight_ref, s32[2,8192]{1,0:T(2,128)} %get-tuple-element.54.lead_nbr_ref, f32[2,8192]{1,0:T(2,128)} %get-tuple-element.52.lead_weight_ref, ...), custom_call_target="tpu_custom_call" | custom-call | flops 200000000 | bytes 200000000 | tf_op jit(solution)/shard_map/pallas_call | solution.py:403
  138.5 2.5 %fusion.7 = (f32[32,1,16,256]{3,2,1,0:T(8,128)S(1)}, f32[32,1,16,256]{3,2,1,0:T(8,128)S(1)}, f32[32,1,16,256]{3,2,1,0:T(8,128)S(1)}, f32[32,1,16,256]{3,2,1,0:T(8,128)}) fusion(f32[32,4,16,256]{3,2,1,0:T(8,128)} %bitcast.22), kind=kLoop, calls=%fused_computation.61 | loop fusion | bytes 4194304 | tf_op jit(solution)/shard_map/slice | solution.py:343
  141.0 0.9 copy.32
  141.9 0.9 copy.33
  142.7 0.9 copy.34
  143.6 28.9 %shard_map.133 = (f32[2,80,8192]{2,1,0:T(8,128)}, f32[512,256]{1,0:T(8,128)}) custom-call(s32[2048]{0:T(1024)} %cell_ref.1, s32[2048,1]{1,0:T(8,128)} %copy.27.row_col_ref, s32[1,2048]{1,0:T(1,128)} %bitcast.32, s32[2048,1]{1,0:T(8,128)} %copy.28.col_ref, f32[512,256]{1,0:T(8,128)} %bitcast.29, f32[2,8192,128]{2,1,0:T(8,128)} %shard_map.132.mixed_ref), custom_call_target="tpu_custom_call" | custom-call | tf_op jit(solution)/shard_map/pallas_call | solution.py:419
  172.5 35.8 %shard_map.134 = (f32[16,256]{1,0:T(8,128)}, f32[16,256]{1,0:T(8,128)}) custom-call(f32[512,256]{1,0:T(8,128)} %get-tuple-element.14.sums_ref, f32[16,256]{1,0:T(8,128)} %thick_ref.1, f32[128,1024]{1,0:T(8,128)} %bitcast.23, f32[128,1024]{1,0:T(8,128)} %bitcast.24, f32[128,1024]{1,0:T(8,128)} %bitcast.25), custom_call_target="tpu_custom_call" | custom-call | tf_op jit(solution)/shard_map/pallas_call | solution.py:437
  208.3 1.3 copy.37
  209.6 1.3 copy.38
  (41 shorter events, 2.4 us)
Async XLA Ops:
  7.2 17.4 %copy-start.5 = (f32[16,256]{1,0:T(8,128)S(1)}, f32[16,256]{1,0:T(8,128)}, u32[]{:S(2)}) copy-start(f32[16,256]{1,0:T(8,128)} %thick_ref.1) | copy-start | bytes 49156
  7.2 17.4 %copy-start.8 = (f32[16,256]{1,0:T(8,128)S(1)}, f32[16,256]{1,0:T(8,128)}, u32[]{:S(2)}) copy-start(f32[16,256]{1,0:T(8,128)} %param.19) | copy-start | bytes 49156
  7.2 17.4 %copy-start.7 = (f32[16,256]{1,0:T(8,128)S(1)}, f32[16,256]{1,0:T(8,128)}, u32[]{:S(2)}) copy-start(f32[16,256]{1,0:T(8,128)} %param.20) | copy-start | bytes 49156
  7.2 17.4 %copy-start.6 = (f32[16,256]{1,0:T(8,128)S(1)}, f32[16,256]{1,0:T(8,128)}, u32[]{:S(2)}) copy-start(f32[16,256]{1,0:T(8,128)} %param.21) | copy-start | bytes 49156
  7.2 18.1 %copy-start = (f32[6,8192]{1,0:T(8,128)S(1)}, f32[6,8192]{1,0:T(8,128)}, u32[]{:S(2)}) copy-start(f32[6,8192]{1,0:T(8,128)} %param.12) | copy-start | bytes 589828
  7.2 18.1 %copy-start.1 = (s32[6,8192]{1,0:T(8,128)S(1)}, s32[6,8192]{1,0:T(8,128)}, u32[]{:S(2)}) copy-start(s32[6,8192]{1,0:T(8,128)} %param.13) | copy-start | bytes 589828
  7.2 22.0 %copy-start.9 = (s32[2048,1]{0,1:T(1,128)S(1)}, s32[2048,1]{0,1:T(1,128)}, u32[]{:S(2)}) copy-start(s32[2048,1]{0,1:T(1,128)} %param.16) | copy-start | bytes 24580
  7.2 22.0 %copy-start.10 = (s32[2048]{0:T(1024)S(1)}, s32[2048]{0:T(1024)}, u32[]{:S(2)}) copy-start(s32[2048]{0:T(1024)} %param.17) | copy-start | bytes 24580
  7.2 131.2 %all-gather.3.cloned.1.call-start = ((), (), s32[]{:S(2)}) async-start(), calls=%async_computation | async-start | bytes 2162688 | tf_op jit(solution)/shard_map/all_gather | solution.py:338
  19.5 54.4 %collective-permute-start = (f32[2,80,1024]{2,1,0:T(8,128)}, f32[2,80,1024]{2,1,0:T(8,128)S(1)}, u32[]{:S(2)}, u32[]{:S(2)}) collective-permute-start(f32[2,80,1024]{2,1,0:T(8,128)} %get-tuple-element.11), channel_id=1, source_target_pairs={{0,1},{1,2},{2,3},{3,4},{4,5},{5,6},{6,7},{7,0},{8,9},{9,10},{10,1... | collective-permute-start | bytes 1966088 | tf_op jit(solution)/shard_map/ppermute | solution.py:359
  21.6 52.3 %collective-permute-start.1 = (f32[2,80,1024]{2,1,0:T(8,128)}, f32[2,80,1024]{2,1,0:T(8,128)S(1)}, u32[]{:S(2)}, u32[]{:S(2)}) collective-permute-start(f32[2,80,1024]{2,1,0:T(8,128)} %get-tuple-element.12), channel_id=1, source_target_pairs={{1,0},{2,1},{3,2},{4,3},{5,4},{6,5},{7,6},{0,7},{9,8},{10,9},{11,1... | collective-permute-start | bytes 1966088 | tf_op jit(solution)/shard_map/ppermute | solution.py:360
  29.2 42.7 %copy-start.4 = (s32[2048]{0:T(1024)}, s32[2048]{0:T(1024)S(1)}, u32[]{:S(2)}) copy-start(s32[2048]{0:T(1024)S(1)} %get-tuple-element.57) | copy-start | bytes 24580
  73.9 0.9 copy-start.2
  73.9 1.0 copy-start.3
Sparse Core Ops, SparseCore 0:
  25.4 61.1 all-gather.2
